TPU v7x, 512 devices: a whole 4x8x8 slice. The times are simulated.
512 devices in a mesh: dp: 64 (over y, z), tower: 8 (over x, core).
Axes of the slice: x: 4, y: 8, z: 8, core: 2. Of those that a mesh axis runs over, the one named last changes fastest.
Arguments:
- rep: bfloat16 [16384, 2048], P('dp', 'tower'), may hold values from -6 to 6
- arm_ids: int32 [16384], P('dp'), may hold values from 0 to 63, as said below
- outcome: bfloat16 [16384], P('dp'), may hold values from -6 to 6
- weight: bfloat16 [16384], P('dp'), may hold values from 0.5 to 4
- w_hidden: bfloat16 [64, 2048, 2048], P('dp', None, 'tower'), may hold values from -0.125 to 0.125
- b_hidden: float32 [64, 2048], P('dp', 'tower'), may hold values from -3 to 3
- w_head: float32 [64, 2048], P('dp', 'tower'), may hold values from -0.125 to 0.125
- b_head: float32 [64], P('dp'), may hold values from -4 to 4
Outputs:
- grad_hidden: float32 [64, 2048, 2048], P('dp', None, 'tower')
- grad_hidden_bias: float32 [64, 2048], P('dp', 'tower')
- grad_head: float32 [64, 2048], P('dp', 'tower')
- grad_head_bias: float32 [64], P('dp')
- grad_rep: bfloat16 [16384, 2048], P('dp', 'tower')
- predicted: bfloat16 [16384], P('dp')
Inputs may be any that keep to these rules, and one draw needn't show every extreme that they name: `arm_ids`: among the 256 rows of one index of dp at most 14 name one arm, and in every draw some index has an arm named exactly 14 times; over all 16384 rows at most 512 name one arm, and in every draw some arm is named exactly 512 times.
All inputs are finite; a program needn't handle non-finite values.
Results may differ from a plain program's by a relative error of at most 0.019.
Values may be sent and summed in bfloat16 or wider, within the bound.
No kernel may reach another device: no remote copies, remote signals or barrier semaphores. Data moves between devices by JAX's collectives and lax.ppermute only.
A program may use at most 64 MiB of HBM per device.

v0:
```python
import jax
import jax.numpy as jnp
from jax import lax
from jax.sharding import PartitionSpec as P


def arm_slots(arm_ids, arm_count, slot_depth):
    arm_labels = jnp.arange(arm_count, dtype=jnp.int32)
    one_hot = (arm_ids[:, None] == arm_labels[None, :]).astype(jnp.int32)
    arm_rank = jnp.sum(jnp.cumsum(one_hot, axis=0) * one_hot, axis=1) - 1
    return arm_ids * slot_depth + arm_rank


def fill_slots(values, slot_index, slot_total):
    row_count = values.shape[0]
    source_row = (
        jnp.full((slot_total,), row_count, jnp.int32)
        .at[slot_index]
        .set(jnp.arange(row_count, dtype=jnp.int32))
    )
    padded_rows = jnp.concatenate(
        [values, jnp.zeros((1,) + values.shape[1:], values.dtype)], axis=0
    )
    return padded_rows[source_row]


def tower_step(inputs, targets, weights, matrix, bias_cols, head_cols, head_bias):
    pre_act = jnp.dot(inputs, matrix, preferred_element_type=jnp.float32) + bias_cols
    sigmoid_pre = jax.nn.sigmoid(pre_act)
    activation = pre_act * sigmoid_pre
    pred_share = jnp.sum(activation * head_cols, axis=1)
    full_pred = lax.psum(pred_share, "tower") + head_bias
    resid_grad = weights * (full_pred - targets)
    pre_grad = resid_grad[:, None] * head_cols * sigmoid_pre * (1.0 + pre_act * (1.0 - sigmoid_pre))
    pre_grad_half = pre_grad.astype(jnp.bfloat16)
    grad_matrix = lax.dot_general(
        inputs, pre_grad_half, (((0,), (0,)), ((), ())), preferred_element_type=jnp.float32
    )
    grad_bias = jnp.sum(pre_grad, axis=0)
    grad_vector = jnp.sum(resid_grad[:, None] * activation, axis=0)
    grad_scalar = jnp.sum(resid_grad)
    return (full_pred, pre_grad_half, grad_matrix, grad_bias, grad_vector, grad_scalar)


def body(rep, arm_ids, outcome, weight, w_hidden, b_hidden, w_head, b_head):
    arm_count = lax.axis_size("dp")
    row_count = arm_ids.shape[0]
    slot_depth = 7 * (row_count // (2 * arm_count))
    slot_total = arm_count * slot_depth
    slot_index = arm_slots(arm_ids, arm_count, slot_depth)
    side_data = fill_slots(jnp.stack([outcome, weight], axis=1), slot_index, slot_total).reshape(
        arm_count, slot_depth, 2
    )
    matrix = w_hidden[0]
    bias_cols = b_hidden[0]
    head_cols = w_head[0]
    head_bias = b_head[0]
    wide_rep = lax.all_gather(rep, "tower", axis=1, tiled=True)
    wide_slots = fill_slots(wide_rep, slot_index, slot_total).reshape(
        arm_count, slot_depth, wide_rep.shape[1]
    )
    arrived, arrived_side = (
        lax.all_to_all(wide_slots, "dp", split_axis=0, concat_axis=0, tiled=True),
        lax.all_to_all(side_data, "dp", split_axis=0, concat_axis=0, tiled=True),
    )
    slot_rows = arrived.reshape(slot_total, arrived.shape[2])
    arrived_side = arrived_side.reshape(slot_total, 2).astype(jnp.float32)
    targets = arrived_side[:, 0]
    weights = arrived_side[:, 1]
    full_pred, pre_grad_half, grad_matrix, grad_bias, grad_vector, grad_scalar = tower_step(
        slot_rows, targets, weights, matrix, bias_cols, head_cols, head_bias
    )
    pred_half = full_pred.astype(jnp.bfloat16)
    partial_full = lax.dot_general(
        pre_grad_half, matrix, (((1,), (1,)), ((), ())), preferred_element_type=jnp.float32
    ).astype(jnp.bfloat16)
    full_width = partial_full.shape[1]
    returned, pred_back = (
        lax.all_to_all(
            partial_full.reshape(arm_count, slot_depth, full_width),
            "dp",
            split_axis=0,
            concat_axis=0,
            tiled=True,
        ),
        lax.all_to_all(
            pred_half.reshape(arm_count, slot_depth), "dp", split_axis=0, concat_axis=0, tiled=True
        ),
    )
    row_partial = returned.reshape(slot_total, full_width)[slot_index]
    grad_rep = lax.psum_scatter(
        row_partial.astype(jnp.float32).astype(jnp.bfloat16),
        "tower",
        scatter_dimension=1,
        tiled=True,
    )
    predicted = pred_back.reshape(slot_total)[slot_index]
    return (
        grad_matrix[None],
        grad_bias[None],
        grad_vector[None],
        grad_scalar.reshape(1),
        grad_rep,
        predicted,
    )


def solution(mesh):
    return jax.shard_map(
        body,
        mesh=mesh,
        in_specs=(
            P("dp", "tower"),
            P("dp"),
            P("dp"),
            P("dp"),
            P("dp", None, "tower"),
            P("dp", "tower"),
            P("dp", "tower"),
            P("dp"),
        ),
        out_specs=(
            P("dp", None, "tower"),
            P("dp", "tower"),
            P("dp", "tower"),
            P("dp"),
            P("dp", "tower"),
            P("dp"),
        ),
        check_vma=False,
    )
```

profile of v0, /device:TPU:8, one launch (start us, length us, event | category | flops | bytes accessed | tf_op | source)
XLA Modules:
  0.0 430.2 jit_solution(11687043676716487167)
XLA Ops:
  7.2 0.7 all-gather.2.cloned.1.call-update
  7.9 0.7 fusion.7
  9.4 0.7 stack.10
  10.1 0.7 stack.9
  11.0 0.8 fusion.6
  11.7 0.7 compare_select_fusion.1
  12.4 1.4 scatter_custom_fusion
  13.9 2.4 gather_fusion.1
  16.6 0.7 copy.27
  17.2 16.6 %all-to-all-start.1 = ((bf16[64,14,2]{1,2,0:T(2,128)(2,1)}), bf16[64,14,2]{1,2,0:T(2,128)(2,1)S(1)}, u32[]{:S(2)}, u32[]{:S(2)}) async-start(bf16[64,14,2]{1,2,0:T(2,128)(2,1)} %copy.27), calls=%async_computation.1 | async-start | bytes 65536 | tf_op jit(solution)/shard_map/all_to_all | solution.py:64
  33.8 9.6 %all-gather.2.cloned.1.call-done = bf16[256,2048]{1,0:T(8,128)(2,1)} async-done(((bf16[256,256]{1,0:T(8,128)(2,1)}), bf16[256,2048]{1,0:T(8,128)(2,1)}) %all-gather.2.cloned.1.call-update) | async-done | bytes 1048592 | tf_op jit(solution)/shard_map/all_gather | solution.py:58
  43.4 1.3 concatenate.6
  44.7 5.0 %gather_fusion = bf16[896,2048]{1,0:T(8,128)(2,1)} fusion(bf16[257,2048]{1,0:T(8,128)(2,1)S(1)} %concatenate.6, s32[1024]{0:T(1024)S(1)} %pad_clamp_fusion.1), kind=kCustom, calls=%fused_computation | custom fusion | bytes 7343616 | tf_op jit(solution)/shard_map/gather | solution.py:24
  49.8 6.0 %reshape.59 = bf16[64,14,2048]{2,1,0:T(8,128)(2,1)} reshape(bf16[896,2048]{1,0:T(8,128)(2,1)} %gather_fusion) | data formatting | bytes 7340032 | tf_op jit(solution)/shard_map/reshape | solution.py:59
  55.8 13.6 %all-to-all-start = ((bf16[64,14,2048]{2,1,0:T(8,128)(2,1)}), bf16[64,14,2048]{2,1,0:T(8,128)(2,1)}, u32[]{:S(2)}, u32[]{:S(2)}) async-start(bf16[64,14,2048]{2,1,0:T(8,128)(2,1)} %reshape.59), calls=%async_computation | async-start | bytes 8388608 | tf_op jit(solution)/shard_map/all_to_all | solution.py:63
  70.4 127.5 %all-to-all-done = bf16[64,14,2048]{2,1,0:T(8,128)(2,1)} async-done(((bf16[64,14,2048]{2,1,0:T(8,128)(2,1)}), bf16[64,14,2048]{2,1,0:T(8,128)(2,1)}, u32[]{:S(2)}, u32[]{:S(2)}) %all-to-all-start) | async-done | bytes 3670048 | tf_op jit(solution)/shard_map/all_to_all | solution.py:63
  197.9 5.8 %reshape.60 = bf16[896,2048]{1,0:T(8,128)(2,1)} reshape(bf16[64,14,2048]{2,1,0:T(8,128)(2,1)} %all-to-all-done) | data formatting | bytes 7340032 | tf_op jit(solution)/shard_map/reshape | solution.py:66
  203.8 3.3 multiply_reduce_fusion.1
  207.1 12.4 %psum.7 = f32[896]{0:T(1024)S(1)} all-reduce(f32[896]{0:T(1024)S(1)} %get-tuple-element.13), channel_id=1, replica_groups=mesh['dp'=64,'tower'=8] {'tower'}, use_global_device_ids=true, to_apply=%region_5.6 | all-reduce | flops 896 | bytes 7168 | tf_op jit(solution)/shard_map/psum | solution.py:32
  220.1 3.1 convolution_convert_fusion
  223.2 6.0 %reshape.63 = bf16[64,14,2048]{2,1,0:T(8,128)(2,1)} reshape(bf16[896,2048]{1,0:T(8,128)(2,1)} %convolution_convert_fusion) | data formatting | bytes 7340032 | tf_op jit(solution)/shard_map/reshape | solution.py:80
  229.2 16.0 %all-to-all-start.2 = ((bf16[64,14,2048]{2,1,0:T(8,128)(2,1)}), bf16[64,14,2048]{2,1,0:T(8,128)(2,1)}, u32[]{:S(2)}, u32[]{:S(2)}) async-start(bf16[64,14,2048]{2,1,0:T(8,128)(2,1)} %reshape.63), calls=%async_computation.2 | async-start | bytes 8388608 | tf_op jit(solution)/shard_map/all_to_all | solution.py:79
  245.4 123.7 %all-to-all-done.2 = bf16[64,14,2048]{2,1,0:T(8,128)(2,1)} async-done(((bf16[64,14,2048]{2,1,0:T(8,128)(2,1)}), bf16[64,14,2048]{2,1,0:T(8,128)(2,1)}, u32[]{:S(2)}, u32[]{:S(2)}) %all-to-all-start.2) | async-done | bytes 3670048 | tf_op jit(solution)/shard_map/all_to_all | solution.py:79
  369.1 6.0 %reshape.64 = bf16[896,2048]{1,0:T(8,128)(2,1)} reshape(bf16[64,14,2048]{2,1,0:T(8,128)(2,1)} %all-to-all-done.2) | data formatting | bytes 7340032 | tf_op jit(solution)/shard_map/reshape | solution.py:90
  375.1 5.9 %gather_fusion.2 = bf16[256,2048]{1,0:T(8,128)(2,1)} fusion(bf16[896,2048]{1,0:T(8,128)(2,1)} %reshape.64, s32[1024]{0:T(1024)S(1)} %pad_clamp_fusion), kind=kCustom, calls=%fused_computation.2 | custom fusion | bytes 2098176 | tf_op jit(solution)/shard_map/gather | solution.py:90
  380.9 0.8 all_to_all.20
  381.7 13.4 %all-to-all-start.3 = ((bf16[64,1,14]{2,1,0:T(2,128)(2,1)}), bf16[64,1,14]{2,1,0:T(2,128)(2,1)S(1)}, u32[]{:S(2)}, u32[]{:S(2)}) async-start(bf16[64,1,14]{2,1,0:T(2,128)(2,1)} %all_to_all.20), calls=%async_computation.4 | async-start | bytes 65536 | tf_op jit(solution)/shard_map/all_to_all | solution.py:86
  395.1 4.9 %convolution_bitcast_fusion = f32[1,2048,256]{2,1,0:T(8,128)} fusion(bf16[896,2048]{1,0:T(8,128)(2,1)} %reshape.60, f32[896,256]{1,0:T(8,128)S(1)} %get-tuple-element.14, f32[896]{0:T(1024)S(1)} %get-tuple-element.11, f32[256]{0:T(256)S(1)} %bitcast.41), kind=kOutput, calls=%fused_computation.6 | convolution fusion | flops 941817856 | bytes 6689280 | tf_op jit(solution)/shard_map/dot_general | solution.py:36
  400.0 1.1 multiply_reduce_fusion
  401.1 5.0 %all-to-all-done.3 = bf16[64,1,14]{2,1,0:T(2,128)(2,1)S(1)} async-done(((bf16[64,1,14]{2,1,0:T(2,128)(2,1)}), bf16[64,1,14]{2,1,0:T(2,128)(2,1)S(1)}, u32[]{:S(2)}, u32[]{:S(2)}) %all-to-all-start.3) | async-done | bytes 1824 | tf_op jit(solution)/shard_map/all_to_all | solution.py:86
  406.3 2.4 gather_fusion.3
  408.8 14.5 %reduce-scatter.2.cloned.1.call-done = bf16[256,256]{1,0:T(8,128)(2,1)} async-done(((bf16[256,2048]{1,0:T(8,128)(2,1)}), bf16[256,256]{1,0:T(8,128)(2,1)}) %reduce-scatter.2.cloned.1.call-update) | async-done | bytes 131088 | tf_op jit(solution)/shard_map/reduce_scatter | solution.py:91
  (30 shorter events, 2.9 us)
Async XLA Ops:
  7.2 196.6 %copy-start = (bf16[1,2048,256]{2,1,0:T(8,128)(2,1)S(1)}, bf16[1,2048,256]{2,1,0:T(8,128)(2,1)}, u32[]{:S(2)}) copy-start(bf16[1,2048,256]{2,1,0:T(8,128)(2,1)} %param.12) | copy-start | bytes 3145732
  7.2 36.3 %all-gather.2.cloned.1.call-start = ((), (), s32[]{:S(2)}) async-start(), calls=%async_computation.5 | async-start | bytes 1179648 | tf_op jit(solution)/shard_map/all_gather | solution.py:58
  17.2 38.5 %all-to-all-start.1 = ((bf16[64,14,2]{1,2,0:T(2,128)(2,1)}), bf16[64,14,2]{1,2,0:T(2,128)(2,1)S(1)}, u32[]{:S(2)}, u32[]{:S(2)}) async-start(bf16[64,14,2]{1,2,0:T(2,128)(2,1)} %copy.27), calls=%async_computation.1 | async-start | bytes 65536 | tf_op jit(solution)/shard_map/all_to_all | solution.py:64
  55.8 142.2 %all-to-all-start = ((bf16[64,14,2048]{2,1,0:T(8,128)(2,1)}), bf16[64,14,2048]{2,1,0:T(8,128)(2,1)}, u32[]{:S(2)}, u32[]{:S(2)}) async-start(bf16[64,14,2048]{2,1,0:T(8,128)(2,1)} %reshape.59), calls=%async_computation | async-start | bytes 8388608 | tf_op jit(solution)/shard_map/all_to_all | solution.py:63
  70.4 133.4 %copy-start.1 = (f32[1,256]{1,0:T(1,128)S(1)}, f32[1,256]{1,0:T(1,128)}, u32[]{:S(2)}) copy-start(f32[1,256]{1,0:T(1,128)} %param.14) | copy-start | bytes 3076
  70.4 133.4 %copy-start.2 = (f32[1,256]{1,0:T(1,128)S(1)}, f32[1,256]{1,0:T(1,128)}, u32[]{:S(2)}) copy-start(f32[1,256]{1,0:T(1,128)} %param.13) | copy-start | bytes 3076
  229.2 139.9 %all-to-all-start.2 = ((bf16[64,14,2048]{2,1,0:T(8,128)(2,1)}), bf16[64,14,2048]{2,1,0:T(8,128)(2,1)}, u32[]{:S(2)}, u32[]{:S(2)}) async-start(bf16[64,14,2048]{2,1,0:T(8,128)(2,1)} %reshape.63), calls=%async_computation.2 | async-start | bytes 8388608 | tf_op jit(solution)/shard_map/all_to_all | solution.py:79
  245.2 178.2 %reduce-scatter.2.cloned.1.call-start = ((), (), s32[]{:S(2)}) async-start(), calls=%async_computation.6 | async-start | bytes 1179648 | tf_op jit(solution)/shard_map/reduce_scatter | solution.py:91
  381.7 24.4 %all-to-all-start.3 = ((bf16[64,1,14]{2,1,0:T(2,128)(2,1)}), bf16[64,1,14]{2,1,0:T(2,128)(2,1)S(1)}, u32[]{:S(2)}, u32[]{:S(2)}) async-start(bf16[64,1,14]{2,1,0:T(2,128)(2,1)} %all_to_all.20), calls=%async_computation.4 | async-start | bytes 65536 | tf_op jit(solution)/shard_map/all_to_all | solution.py:86
Sparse Core Ops, SparseCore 0:
  10.1 33.2 all-gather.1
  381.1 42.2 reduce-scatter.1
where the time goes:
time: 431 us; the launch traced here: 430 us
  waiting for transfers between devices  281 us (65%)
  starting transfers between devices  59.7 us (14%)
  local copies, waits for them, and re-layouts  46.2 us (11%)
  between operations  14.8 us (3%)
  blocking collectives  12.4 us (3%)
  matrix products  11.3 us (3%)
  other arithmetic  4.59 us (1%)
    all_to_all x1, waiting for transfers between devices, body(): lax.all_to_all(wide_slots, 'dp', split_axis=0, concat_axis=0, tiled=True)  128 us
    all_to_all x1, waiting for transfers between devices, body(): lax.all_to_all(partial_full.reshape(arm_count, slot_depth, full_width), '...  124 us
    all_to_all x1, starting transfers between devices, body(): lax.all_to_all(side_data, 'dp', split_axis=0, concat_axis=0, tiled=True)  16.6 us
    all_to_all x1, starting transfers between devices, body(): lax.all_to_all(partial_full.reshape(arm_count, slot_depth, full_width), '...  16 us
    reduce_scatter x1, waiting for transfers between devices, body(): lax.psum_scatter(row_partial.astype(jnp.float32).astype(jnp.bfloat16), 't...  14.5 us
    all_to_all x1, starting transfers between devices, body(): lax.all_to_all(wide_slots, 'dp', split_axis=0, concat_axis=0, tiled=True)  13.6 us
    all_to_all x1, starting transfers between devices, body(): lax.all_to_all(pred_half.reshape(arm_count, slot_depth), 'dp', split_axis...  13.4 us
    psum x1, blocking collectives, tower_step(): full_pred = lax.psum(pred_share, 'tower') + head_bias  12.4 us
  transfers between devices with their start and end apart: 6, of which 5 were waited for; matrix products, arithmetic and copies ran while one was open for 7% of the time, Pallas kernels for 0%

commit v1 on v0

--- a/solution.py
+++ b/solution.py
@@ -2,6 +2,24 @@
 import jax.numpy as jnp
 from jax import lax
 from jax.sharding import PartitionSpec as P
+
+
+def ring_gather(array, axis, dim):
+    ways, here, step = (lax.axis_size(axis), lax.axis_index(axis), array.shape[dim])
+    lengths = [n * ways if d == dim else n for d, n in enumerate(array.shape)]
+    full = lax.dynamic_update_slice_in_dim(
+        jnp.zeros(lengths, array.dtype), array, here * step, axis=dim
+    )
+    going_up = going_down = array
+    for far in range(1, ways // 2 + 1):
+        going_up = lax.ppermute(going_up, axis, [(d, (d + 1) % ways) for d in range(ways)])
+        full = lax.dynamic_update_slice_in_dim(full, going_up, (here - far) % ways * step, axis=dim)
+        if 2 * far < ways:
+            going_down = lax.ppermute(going_down, axis, [(d, (d - 1) % ways) for d in range(ways)])
+            full = lax.dynamic_update_slice_in_dim(
+                full, going_down, (here + far) % ways * step, axis=dim
+            )
+    return full
 
 
 def arm_slots(arm_ids, arm_count, slot_depth):
@@ -55,7 +73,7 @@
     bias_cols = b_hidden[0]
     head_cols = w_head[0]
     head_bias = b_head[0]
-    wide_rep = lax.all_gather(rep, "tower", axis=1, tiled=True)
+    wide_rep = ring_gather(rep, "tower", 1)
     wide_slots = fill_slots(wide_rep, slot_index, slot_total).reshape(
         arm_count, slot_depth, wide_rep.shape[1]
     )

time: 431 us -> 457 us (1.060)
  blocking collectives: 12.4 us -> 32.9 us
  starting transfers between devices: 59.7 us -> 79.5 us
  waiting for transfers between devices: 281 us -> 267 us
    reduce_scatter x1, waiting for transfers between devices: 14.5 us -> 36.2 us  [body(): lax.psum_scatter(row_partial.astype(jnp.float32).astype(jnp.bfloat16), 't...]
    psum x1, blocking collectives: 12.4 us -> 32.9 us  [tower_step(): full_pred = lax.psum(pred_share, 'tower') + head_bias]
    all_to_all x1, waiting for transfers between devices: 128 us -> 108 us  [body(): lax.all_to_all(wide_slots, 'dp', split_axis=0, concat_axis=0, tiled=True)]
    all_to_all x1, waiting for transfers between devices: 124 us -> 107 us  [body(): lax.all_to_all(partial_full.reshape(arm_count, slot_depth, full_width), '...]
    all_to_all x1, starting transfers between devices: 13.4 us -> 26 us  [body(): lax.all_to_all(pred_half.reshape(arm_count, slot_depth), 'dp', split_axis...]
    ppermute x0 -> x7, waiting for transfers between devices: none -> 10.5 us  [the longest x4 10.3 us: ring_gather(): lax.ppermute(going_up, axis, [(d, (d + 1) % ways) for d in range(ways)])]
    all_gather x1 -> x0, waiting for transfers between devices: 9.63 us -> none  [body(): wide_rep = lax.all_gather(rep, 'tower', axis=1, tiled=True)]
    ppermute x0 -> x7, starting transfers between devices: none -> 9.17 us  [the longest x3 9.13 us: ring_gather(): lax.ppermute(going_down, axis, [(d, (d - 1) % ways) for d in range(ways)])]
  transfers between devices with their start and end apart: 6 -> 12, of which waited for: 5 -> 8; matrix products, arithmetic and copies ran while one was open for 7% -> 7% of each run, Pallas kernels for 0% -> 0%
where the time goes in v1:
time: 457 us; the launch traced here: 456 us
  waiting for transfers between devices  267 us (58%)
  starting transfers between devices  79.5 us (17%)
  local copies, waits for them, and re-layouts  45.2 us (10%)
  blocking collectives  32.9 us (7%)
  between operations  15.1 us (3%)
  matrix products  11.4 us (2%)
  other arithmetic  4.59 us (1%)
    all_to_all x1, waiting for transfers between devices, body(): lax.all_to_all(wide_slots, 'dp', split_axis=0, concat_axis=0, tiled=True)  108 us
    all_to_all x1, waiting for transfers between devices, body(): lax.all_to_all(partial_full.reshape(arm_count, slot_depth, full_width), '...  107 us
    reduce_scatter x1, waiting for transfers between devices, body(): lax.psum_scatter(row_partial.astype(jnp.float32).astype(jnp.bfloat16), 't...  36.2 us
    psum x1, blocking collectives, tower_step(): full_pred = lax.psum(pred_share, 'tower') + head_bias  32.9 us
    all_to_all x1, starting transfers between devices, body(): lax.all_to_all(pred_half.reshape(arm_count, slot_depth), 'dp', split_axis...  26 us
    all_to_all x1, starting transfers between devices, body(): lax.all_to_all(side_data, 'dp', split_axis=0, concat_axis=0, tiled=True)  16.6 us
    all_to_all x1, starting transfers between devices, body(): lax.all_to_all(partial_full.reshape(arm_count, slot_depth, full_width), '...  14.6 us
    all_to_all x1, starting transfers between devices, body(): lax.all_to_all(wide_slots, 'dp', split_axis=0, concat_axis=0, tiled=True)  12.9 us
  transfers between devices with their start and end apart: 12, of which 8 were waited for; matrix products, arithmetic and copies ran while one was open for 7% of the time, Pallas kernels for 0%

profile of v1, /device:TPU:8, one launch (start us, length us, event | category | flops | bytes accessed | tf_op | source)
XLA Modules:
  0.0 455.5 jit_solution(14940473951600495516)
XLA Ops:
  7.2 2.9 collective-permute-start.1
  10.2 0.7 fusion.7
  11.7 0.8 fusion.6
  12.5 0.7 compare_select_fusion.1
  13.2 1.4 scatter_custom_fusion
  16.1 2.4 gather_fusion.1
  19.5 16.6 %all-to-all-start.1 = ((bf16[64,14,2]{1,2,0:T(2,128)(2,1)}), bf16[64,14,2]{1,2,0:T(2,128)(2,1)S(1)}, u32[]{:S(2)}, u32[]{:S(2)}) async-start(bf16[64,14,2]{1,2,0:T(2,128)(2,1)} %copy.27), calls=%async_computation.1 | async-start | bytes 65536 | tf_op jit(solution)/shard_map/all_to_all | solution.py:82
  36.4 2.9 collective-permute-start.3
  39.4 2.6 collective-permute-done.2
  42.0 3.2 collective-permute-start.5
  45.3 2.3 collective-permute-done.4
  47.8 5.4 %collective-permute-done.6 = bf16[256,256]{1,0:T(8,128)(2,1)S(1)} collective-permute-done((bf16[256,256]{1,0:T(8,128)(2,1)S(1)}, bf16[256,256]{1,0:T(8,128)(2,1)S(1)}, u32[]{:S(2)}, u32[]{:S(2)}) %collective-permute-start.6) | collective-permute-done | bytes 131104 | tf_op jit(solution)/shard_map/ppermute | solution.py:15
  53.3 5.0 %gather_fusion = bf16[896,2048]{1,0:T(8,128)(2,1)} fusion(bf16[257,2048]{1,0:T(8,128)(2,1)S(1)} %concatenate.6, s32[1024]{0:T(1024)S(1)} %pad_clamp_fusion.1), kind=kCustom, calls=%fused_computation | custom fusion | bytes 7343616 | tf_op jit(solution)/shard_map/gather | solution.py:42
  58.3 6.0 %reshape.59 = bf16[64,14,2048]{2,1,0:T(8,128)(2,1)} reshape(bf16[896,2048]{1,0:T(8,128)(2,1)} %gather_fusion) | data formatting | bytes 7340032 | tf_op jit(solution)/shard_map/reshape | solution.py:77
  64.3 12.9 %all-to-all-start = ((bf16[64,14,2048]{2,1,0:T(8,128)(2,1)}), bf16[64,14,2048]{2,1,0:T(8,128)(2,1)}, u32[]{:S(2)}, u32[]{:S(2)}) async-start(bf16[64,14,2048]{2,1,0:T(8,128)(2,1)} %reshape.59), calls=%async_computation | async-start | bytes 8388608 | tf_op jit(solution)/shard_map/all_to_all | solution.py:81
  78.3 108.4 %all-to-all-done = bf16[64,14,2048]{2,1,0:T(8,128)(2,1)} async-done(((bf16[64,14,2048]{2,1,0:T(8,128)(2,1)}), bf16[64,14,2048]{2,1,0:T(8,128)(2,1)}, u32[]{:S(2)}, u32[]{:S(2)}) %all-to-all-start) | async-done | bytes 3670048 | tf_op jit(solution)/shard_map/all_to_all | solution.py:81
  186.7 5.8 %reshape.60 = bf16[896,2048]{1,0:T(8,128)(2,1)} reshape(bf16[64,14,2048]{2,1,0:T(8,128)(2,1)} %all-to-all-done) | data formatting | bytes 7340032 | tf_op jit(solution)/shard_map/reshape | solution.py:84
  192.6 3.3 multiply_reduce_fusion.1
  195.8 32.9 %psum.7 = f32[896]{0:T(1024)S(1)} all-reduce(f32[896]{0:T(1024)S(1)} %get-tuple-element.13), channel_id=1, replica_groups=mesh['dp'=64,'tower'=8] {'tower'}, use_global_device_ids=true, to_apply=%region_5.6 | all-reduce | flops 896 | bytes 7168 | tf_op jit(solution)/shard_map/psum | solution.py:50
  229.4 3.1 convolution_convert_fusion
  232.5 6.0 %reshape.63 = bf16[64,14,2048]{2,1,0:T(8,128)(2,1)} reshape(bf16[896,2048]{1,0:T(8,128)(2,1)} %convolution_convert_fusion) | data formatting | bytes 7340032 | tf_op jit(solution)/shard_map/reshape | solution.py:98
  238.5 14.6 %all-to-all-start.2 = ((bf16[64,14,2048]{2,1,0:T(8,128)(2,1)}), bf16[64,14,2048]{2,1,0:T(8,128)(2,1)}, u32[]{:S(2)}, u32[]{:S(2)}) async-start(bf16[64,14,2048]{2,1,0:T(8,128)(2,1)} %reshape.63), calls=%async_computation.2 | async-start | bytes 8388608 | tf_op jit(solution)/shard_map/all_to_all | solution.py:97
  253.3 106.7 %all-to-all-done.2 = bf16[64,14,2048]{2,1,0:T(8,128)(2,1)} async-done(((bf16[64,14,2048]{2,1,0:T(8,128)(2,1)}), bf16[64,14,2048]{2,1,0:T(8,128)(2,1)}, u32[]{:S(2)}, u32[]{:S(2)}) %all-to-all-start.2) | async-done | bytes 3670048 | tf_op jit(solution)/shard_map/all_to_all | solution.py:97
  360.0 6.0 %reshape.64 = bf16[896,2048]{1,0:T(8,128)(2,1)} reshape(bf16[64,14,2048]{2,1,0:T(8,128)(2,1)} %all-to-all-done.2) | data formatting | bytes 7340032 | tf_op jit(solution)/shard_map/reshape | solution.py:108
  366.0 5.9 %gather_fusion.2 = bf16[256,2048]{1,0:T(8,128)(2,1)} fusion(bf16[896,2048]{1,0:T(8,128)(2,1)} %reshape.64, s32[1024]{0:T(1024)S(1)} %pad_clamp_fusion), kind=kCustom, calls=%fused_computation.2 | custom fusion | bytes 2098176 | tf_op jit(solution)/shard_map/gather | solution.py:108
  371.9 0.8 all_to_all.20
  372.6 26.0 %all-to-all-start.3 = ((bf16[64,1,14]{2,1,0:T(2,128)(2,1)}), bf16[64,1,14]{2,1,0:T(2,128)(2,1)S(1)}, u32[]{:S(2)}, u32[]{:S(2)}) async-start(bf16[64,1,14]{2,1,0:T(2,128)(2,1)} %all_to_all.20), calls=%async_computation.4 | async-start | bytes 65536 | tf_op jit(solution)/shard_map/all_to_all | solution.py:104
  398.7 4.9 %convolution_bitcast_fusion = f32[1,2048,256]{2,1,0:T(8,128)} fusion(bf16[896,2048]{1,0:T(8,128)(2,1)} %reshape.60, f32[896,256]{1,0:T(8,128)S(1)} %get-tuple-element.14, f32[896]{0:T(1024)S(1)} %get-tuple-element.11, f32[256]{0:T(256)S(1)} %bitcast.41), kind=kOutput, calls=%fused_computation.6 | convolution fusion | flops 941817856 | bytes 6689280 | tf_op jit(solution)/shard_map/dot_general | solution.py:54
  403.6 1.1 multiply_reduce_fusion
  404.7 5.0 %all-to-all-done.3 = bf16[64,1,14]{2,1,0:T(2,128)(2,1)S(1)} async-done(((bf16[64,1,14]{2,1,0:T(2,128)(2,1)}), bf16[64,1,14]{2,1,0:T(2,128)(2,1)S(1)}, u32[]{:S(2)}, u32[]{:S(2)}) %all-to-all-start.3) | async-done | bytes 1824 | tf_op jit(solution)/shard_map/all_to_all | solution.py:104
  410.0 2.4 gather_fusion.3
  412.4 36.2 %reduce-scatter.2.cloned.1.call-done = bf16[256,256]{1,0:T(8,128)(2,1)} async-done(((bf16[256,2048]{1,0:T(8,128)(2,1)}), bf16[256,256]{1,0:T(8,128)(2,1)}) %reduce-scatter.2.cloned.1.call-update) | async-done | bytes 131088 | tf_op jit(solution)/shard_map/reduce_scatter | solution.py:109
  (52 shorter events, 5.3 us)
Async XLA Ops:
  7.2 185.4 %copy-start = (bf16[1,2048,256]{2,1,0:T(8,128)(2,1)S(1)}, bf16[1,2048,256]{2,1,0:T(8,128)(2,1)}, u32[]{:S(2)}) copy-start(bf16[1,2048,256]{2,1,0:T(8,128)(2,1)} %param.12) | copy-start | bytes 3145732
  7.2 29.1 %copy-start.1 = (bf16[256,256]{1,0:T(8,128)(2,1)S(1)}, bf16[256,256]{1,0:T(8,128)(2,1)}, u32[]{:S(2)}) copy-start(bf16[256,256]{1,0:T(8,128)(2,1)} %param.8) | copy-start | bytes 393220
  7.2 29.2 %collective-permute-start = (bf16[256,256]{1,0:T(8,128)(2,1)}, bf16[256,256]{1,0:T(8,128)(2,1)S(1)}, u32[]{:S(2)}, u32[]{:S(2)}) collective-permute-start(bf16[256,256]{1,0:T(8,128)(2,1)} %param.8), channel_id=1, source_target_pairs={{0,1},{1,2},{2,3},{3,4},{4,5},{5,6},{6,7},{7,0},{8,9},{9,10},{10,1... | collective-permute-start | bytes 393224 | tf_op jit(solution)/shard_map/ppermute | solution.py:15
  7.2 29.2 %collective-permute-start.1 = (bf16[256,256]{1,0:T(8,128)(2,1)}, bf16[256,256]{1,0:T(8,128)(2,1)S(1)}, u32[]{:S(2)}, u32[]{:S(2)}) collective-permute-start(bf16[256,256]{1,0:T(8,128)(2,1)} %param.8), channel_id=1, source_target_pairs={{0,7},{1,0},{2,1},{3,2},{4,3},{5,4},{6,5},{7,6},{8,15},{9,8},{10,9... | collective-permute-start | bytes 393224 | tf_op jit(solution)/shard_map/ppermute | solution.py:18
  19.5 44.8 %all-to-all-start.1 = ((bf16[64,14,2]{1,2,0:T(2,128)(2,1)}), bf16[64,14,2]{1,2,0:T(2,128)(2,1)S(1)}, u32[]{:S(2)}, u32[]{:S(2)}) async-start(bf16[64,14,2]{1,2,0:T(2,128)(2,1)} %copy.27), calls=%async_computation.1 | async-start | bytes 65536 | tf_op jit(solution)/shard_map/all_to_all | solution.py:82
  36.4 5.6 %collective-permute-start.2 = (bf16[256,256]{1,0:T(8,128)(2,1)S(1)}, bf16[256,256]{1,0:T(8,128)(2,1)S(1)}, u32[]{:S(2)}, u32[]{:S(2)}) collective-permute-start(bf16[256,256]{1,0:T(8,128)(2,1)S(1)} %collective-permute-done), channel_id=1, source_target_pairs={{0,1},{1,2},{2,3},{3,4},{4,5},{5,6},{6,7},{7,0},{8,9},{9,10},{10,1... | collective-permute-start | bytes 393224 | tf_op jit(solution)/shard_map/ppermute | solution.py:15
  36.4 5.6 %collective-permute-start.3 = (bf16[256,256]{1,0:T(8,128)(2,1)S(1)}, bf16[256,256]{1,0:T(8,128)(2,1)S(1)}, u32[]{:S(2)}, u32[]{:S(2)}) collective-permute-start(bf16[256,256]{1,0:T(8,128)(2,1)S(1)} %collective-permute-done.1), channel_id=1, source_target_pairs={{0,7},{1,0},{2,1},{3,2},{4,3},{5,4},{6,5},{7,6},{8,15},{9,8},{10,9... | collective-permute-start | bytes 393224 | tf_op jit(solution)/shard_map/ppermute | solution.py:18
  42.0 5.6 %collective-permute-start.4 = (bf16[256,256]{1,0:T(8,128)(2,1)S(1)}, bf16[256,256]{1,0:T(8,128)(2,1)S(1)}, u32[]{:S(2)}, u32[]{:S(2)}) collective-permute-start(bf16[256,256]{1,0:T(8,128)(2,1)S(1)} %collective-permute-done.2), channel_id=1, source_target_pairs={{0,1},{1,2},{2,3},{3,4},{4,5},{5,6},{6,7},{7,0},{8,9},{9,10},{10,1... | collective-permute-start | bytes 393224 | tf_op jit(solution)/shard_map/ppermute | solution.py:15
  42.0 5.8 %collective-permute-start.5 = (bf16[256,256]{1,0:T(8,128)(2,1)S(1)}, bf16[256,256]{1,0:T(8,128)(2,1)S(1)}, u32[]{:S(2)}, u32[]{:S(2)}) collective-permute-start(bf16[256,256]{1,0:T(8,128)(2,1)S(1)} %collective-permute-done.3), channel_id=1, source_target_pairs={{0,7},{1,0},{2,1},{3,2},{4,3},{5,4},{6,5},{7,6},{8,15},{9,8},{10,9... | collective-permute-start | bytes 393224 | tf_op jit(solution)/shard_map/ppermute | solution.py:18
  47.6 5.6 %collective-permute-start.6 = (bf16[256,256]{1,0:T(8,128)(2,1)S(1)}, bf16[256,256]{1,0:T(8,128)(2,1)S(1)}, u32[]{:S(2)}, u32[]{:S(2)}) collective-permute-start(bf16[256,256]{1,0:T(8,128)(2,1)S(1)} %collective-permute-done.4), channel_id=1, source_target_pairs={{0,1},{1,2},{2,3},{3,4},{4,5},{5,6},{6,7},{7,0},{8,9},{9,10},{10,1... | collective-permute-start | bytes 393224 | tf_op jit(solution)/shard_map/ppermute | solution.py:15
  64.3 122.4 %all-to-all-start = ((bf16[64,14,2048]{2,1,0:T(8,128)(2,1)}), bf16[64,14,2048]{2,1,0:T(8,128)(2,1)}, u32[]{:S(2)}, u32[]{:S(2)}) async-start(bf16[64,14,2048]{2,1,0:T(8,128)(2,1)} %reshape.59), calls=%async_computation | async-start | bytes 8388608 | tf_op jit(solution)/shard_map/all_to_all | solution.py:81
  78.2 114.3 %copy-start.2 = (f32[1,256]{1,0:T(1,128)S(1)}, f32[1,256]{1,0:T(1,128)}, u32[]{:S(2)}) copy-start(f32[1,256]{1,0:T(1,128)} %param.14) | copy-start | bytes 3076
  78.2 114.3 %copy-start.3 = (f32[1,256]{1,0:T(1,128)S(1)}, f32[1,256]{1,0:T(1,128)}, u32[]{:S(2)}) copy-start(f32[1,256]{1,0:T(1,128)} %param.13) | copy-start | bytes 3076
  238.5 121.5 %all-to-all-start.2 = ((bf16[64,14,2048]{2,1,0:T(8,128)(2,1)}), bf16[64,14,2048]{2,1,0:T(8,128)(2,1)}, u32[]{:S(2)}, u32[]{:S(2)}) async-start(bf16[64,14,2048]{2,1,0:T(8,128)(2,1)} %reshape.63), calls=%async_computation.2 | async-start | bytes 8388608 | tf_op jit(solution)/shard_map/all_to_all | solution.py:97
  253.1 195.6 %reduce-scatter.2.cloned.1.call-start = ((), (), s32[]{:S(2)}) async-start(), calls=%async_computation.5 | async-start | bytes 1179648 | tf_op jit(solution)/shard_map/reduce_scatter | solution.py:109
  372.6 37.1 %all-to-all-start.3 = ((bf16[64,1,14]{2,1,0:T(2,128)(2,1)}), bf16[64,1,14]{2,1,0:T(2,128)(2,1)S(1)}, u32[]{:S(2)}, u32[]{:S(2)}) async-start(bf16[64,1,14]{2,1,0:T(2,128)(2,1)} %all_to_all.20), calls=%async_computation.4 | async-start | bytes 65536 | tf_op jit(solution)/shard_map/all_to_all | solution.py:104
Sparse Core Ops, SparseCore 0:
  372.0 76.6 reduce-scatter.1
